TPU v7x, 128 devices: a whole 4x4x4 slice. The times are simulated.
128 devices in a mesh: inp: 32 (over x, y_lo, z), grp: 4 (over y_hi, core).
Axes of the slice: x: 4, y: 4 (y_hi: 2, y_lo: 2; y = y_hi * 2 + y_lo), z: 4, core: 2. Of those that a mesh axis runs over, the one named last changes fastest.
Arguments:
- raw: bfloat16 [4096, 268288], P(('inp', 'grp')), may hold values from -6 to 6
- steer: int32 [256, 4096], P(None, ('inp', 'grp')), may hold values from 0 to 255
- slot_map: int32 [4096], replicated, may hold values from 0 to 4095, each once
Outputs:
- visibility: float32 [2, 32768, 4096], P(None, ('inp', 'grp'))
- beam_power: float32 [512, 256], P(('inp', 'grp'))
Inputs may be any that keep to these rules, and one draw needn't show every extreme that they name: slot_map is a permutation of the 4096 streams. steer's values matter only modulo 256; a program may carry them between devices in any exact form, several to a word.
All inputs are finite; a program needn't handle non-finite values.
Results may differ from a plain program's by a relative error of at most 0.0069.
Values may be sent and summed in bfloat16 or wider, within the bound.
A program may use at most 128 MiB of HBM per device.

v0:
```python
import math

import jax
import jax.numpy as jnp
from jax import lax
from jax.sharding import PartitionSpec as P

NFFT = 2048
TAPS = 4
PHASES = 256
CH_GRP = 128
ROWS = 64


def prototype():
    pos = jnp.arange(TAPS * NFFT, dtype=jnp.float32) + 0.5
    arg = pos / NFFT - TAPS / 2.0
    window = 0.5 - 0.5 * jnp.cos(2.0 * math.pi * pos / (TAPS * NFFT))
    return (jnp.sinc(arg) * window).reshape(TAPS, NFFT)


def channel_numbers(n_grp, ch_dev):
    sub = NFFT // 2 // n_grp
    order = jnp.arange(CH_GRP * n_grp, dtype=jnp.int32)
    device = order // ch_dev
    inner = order % ch_dev
    return device % n_grp * sub + (sub - CH_GRP) // 2 + device // n_grp * ch_dev + inner


def dft_table(chans):
    sample = jnp.arange(NFFT, dtype=jnp.int32)
    phase = (chans[:, None] * sample[None, :] % NFFT).astype(jnp.float32)
    angle = 2.0 * math.pi * phase / NFFT
    scale = 1.0 / math.sqrt(NFFT)
    return jnp.stack([jnp.cos(angle) * scale, -jnp.sin(angle) * scale]).astype(jnp.bfloat16)


def steering(indices, number, streams):
    phase = (indices * number % PHASES).astype(jnp.float32)
    angle = 2.0 * math.pi * phase / PHASES
    wcos = (jnp.cos(angle) / math.sqrt(streams)).astype(jnp.bfloat16)
    wsin = (jnp.sin(angle) / math.sqrt(streams)).astype(jnp.bfloat16)
    return (wcos, wsin)


def per_device(raw, steer, slot_map):
    n_inp = lax.axis_size("inp")
    n_grp = lax.axis_size("grp")
    count = n_inp * n_grp
    ns_dev, samples = raw.shape
    streams = ns_dev * count
    frames = samples // NFFT - TAPS + 1
    ch_dev = CH_GRP // n_inp
    device = lax.axis_index("inp") * n_grp + lax.axis_index("grp")
    proto = prototype()
    chans = channel_numbers(n_grp, ch_dev)
    table = dft_table(chans)
    view = raw.reshape(ns_dev, frames + TAPS - 1, NFFT)
    acc = jnp.zeros((ns_dev, frames, NFFT), jnp.float32)
    for tap in range(TAPS):
        acc = acc + proto[tap][None, None, :] * view[:, tap : tap + frames, :]
    filtered = acc.astype(jnp.bfloat16)
    spectra = jnp.einsum(
        "rcn,sfn->crsf", table, filtered, preferred_element_type=jnp.float32
    ).astype(jnp.bfloat16)
    outgoing = spectra.reshape(count, ch_dev, 2, ns_dev, frames)
    arrived = lax.all_to_all(outgoing, ("inp", "grp"), split_axis=0, concat_axis=3, tiled=True)
    chan_data = arrived[0]
    numbers = lax.dynamic_slice_in_dim(chans, device * ch_dev, ch_dev, 0)
    permuted = jnp.take(chan_data, slot_map, axis=2)
    left = permuted[:, :, :ROWS].reshape(ch_dev, 2 * ROWS, frames)
    right = permuted.reshape(ch_dev, 2 * streams, frames)
    prod = jnp.einsum("kaf,kbf->kab", left, right, preferred_element_type=jnp.float32)
    real_part = (prod[:, :ROWS, :streams] + prod[:, ROWS:, streams:]) / frames
    imag_part = (prod[:, :ROWS, streams:] - prod[:, ROWS:, :streams]) / frames
    visibility = jnp.stack([real_part, imag_part]).reshape(2, ch_dev * ROWS, streams)
    steer_all = lax.all_gather(steer, ("inp", "grp"), axis=1, tiled=True)
    wcos, wsin = steering(steer_all[None, :, :], numbers[:, None, None], streams)
    real_in = chan_data[:, 0]
    imag_in = chan_data[:, 1]
    beam_re = jnp.einsum(
        "kbs,ksf->kbf", wcos, real_in, preferred_element_type=jnp.float32
    ) + jnp.einsum("kbs,ksf->kbf", wsin, imag_in, preferred_element_type=jnp.float32)
    beam_im = jnp.einsum(
        "kbs,ksf->kbf", wcos, imag_in, preferred_element_type=jnp.float32
    ) - jnp.einsum("kbs,ksf->kbf", wsin, real_in, preferred_element_type=jnp.float32)
    power = jnp.sum(beam_re * beam_re + beam_im * beam_im, axis=2) / frames
    return (visibility, power)


def solution(mesh):
    in_specs = (P(("inp", "grp"), None), P(None, ("inp", "grp")), P())
    out_specs = (P(None, ("inp", "grp"), None), P(("inp", "grp"), None))
    return jax.shard_map(
        per_device, mesh=mesh, in_specs=in_specs, out_specs=out_specs, check_vma=False
    )
```

profile of v0, /device:TPU:1, one launch (start us, length us, event | category | flops | bytes accessed | tf_op | source)
XLA Modules:
  0.0 774.8 jit_solution(2718472671234241515)
XLA Ops:
  7.2 0.2 fusion.36
  7.4 18.9 %multiply_convert_fusion.7 = (bf16[1,512,2048]{2,1,0:T(8,128)(2,1)S(1)}, bf16[1,512,2048]{2,1,0:T(8,128)(2,1)}) fusion(s32[512]{0:T(512)S(1)} %fusion.53), kind=kLoop, calls=%fused_computation.41 | loop fusion | flops 19922944 | bytes 4196352 | tf_op jit(solution)/shard_map/convert
  26.3 25.2 %reshape.199 = bf16[32,131,2048]{2,1,0:T(8,128)(2,1)} reshape(bf16[32,268288]{1,0:T(8,128)(2,1)} %param.3) | data formatting | bytes 34340864 | tf_op jit(solution)/shard_map/reshape | solution.py:58
  51.5 42.6 %convert_bitcast_fusion = bf16[512,2,32,128]{0,3,1,2:T(8,128)(2,1)} fusion(bf16[32,131,2048]{2,1,0:T(8,128)(2,1)} %reshape.199, f32[2048]{0:T(1024)S(1)} %get-tuple-element.5, f32[2048]{0:T(1024)S(1)} %get-tuple-element.6, f32[2048]{0:T(1024)S(1)} %get-tuple-element.7, f32[2048]{0:T(1024)S(1)} %get-tuple-element.4, ...), kind=kOutput, calls=%fused_computation.20 | convolution fusion | flops 17293115392 | bytes 79724544 | tf_op jit(solution)/shard_map/rcn,sfn->crsf/dot_general | solution.py:63
  94.1 14.9 %copy.8 = bf16[512,2,32,128]{3,2,1,0:T(8,128)(2,1)} copy(bf16[512,2,32,128]{0,3,1,2:T(8,128)(2,1)} %convert_bitcast_fusion) | data formatting | bytes 16777216 | tf_op jit(solution)/shard_map/convert_element_type | solution.py:65
  109.0 0.0 copy-start.2
  109.0 12.0 %all-to-all-start = ((bf16[128,4,2,32,128]{4,3,2,1,0:T(8,128)(2,1)}), bf16[128,4,2,32,128]{4,3,2,1,0:T(8,128)(2,1)}, u32[]{:S(2)}, u32[]{:S(2)}) async-start(bf16[128,4,2,32,128]{4,3,2,1,0:T(8,128)(2,1)} %bitcast.63), calls=%async_computation | async-start | bytes 16777216 | tf_op jit(solution)/shard_map/all_to_all | solution.py:67
  121.0 15.5 %all-gather.2.cloned.1.call-start = ((), (), s32[]{:S(2)}) async-start(), calls=%async_computation.1 | async-start | bytes 4227072 | tf_op jit(solution)/shard_map/all_gather | solution.py:77
  136.5 0.0 all-gather.2.cloned.1.call-update
  136.5 0.1 dynamic_slice.3
  136.6 0.0 copy-done.2
  136.7 92.6 %all-to-all-done = bf16[128,4,2,32,128]{4,3,2,1,0:T(8,128)(2,1)} async-done(((bf16[128,4,2,32,128]{4,3,2,1,0:T(8,128)(2,1)}), bf16[128,4,2,32,128]{4,3,2,1,0:T(8,128)(2,1)}, u32[]{:S(2)}, u32[]{:S(2)}) %all-to-all-start) | async-done | bytes 8388640 | tf_op jit(solution)/shard_map/all_to_all | solution.py:67
  229.3 8.5 %copy.9 = bf16[1,4,2,128,32,128]{5,4,3,2,1,0:T(8,128)(2,1)} copy(bf16[1,4,2,128,32,128]{5,4,2,1,3,0:T(8,128)(2,1)} %bitcast.6) | data formatting | bytes 16777216 | tf_op jit(solution)/shard_map/all_to_all | solution.py:67
  237.8 157.3 %all-gather.2.cloned.1.call-done = s32[256,4096]{0,1:T(8,128)} async-done(((s32[256,32]{0,1:T(8,128)}), s32[256,4096]{0,1:T(8,128)}) %all-gather.2.cloned.1.call-update) | async-done | bytes 4194320 | tf_op jit(solution)/shard_map/all_gather | solution.py:77
  395.1 5.7 copy.13
  400.8 0.0 copy-start
  400.8 0.0 copy-start.1
  400.8 67.0 %fusion.11 = f32[4,256,128]{1,2,0:T(8,128)S(1)} fusion(s32[4]{0:T(128)S(1)} %dynamic_slice.3, s32[256,4096]{1,0:T(8,128)} %copy.13, bf16[4,2,4096,128]{3,2,1,0:T(8,128)(2,1)} %bitcast.64), kind=kOutput, calls=%fused_computation.22 | convolution fusion | flops 1140850688 | bytes 8912912 | tf_op jit(solution)/shard_map/kbs,ksf->kbf/dot_general | solution.py:81
  467.8 0.0 copy-done
  467.8 0.0 copy-done.1
  467.8 62.9 %fusion.10 = f32[4,256,128]{1,2,0:T(8,128)S(1)} fusion(s32[4]{0:T(128)S(1)} %dynamic_slice.3, s32[256,4096]{1,0:T(8,128)S(1)} %copy-done.1, bf16[4,2,4096,128]{3,2,1,0:T(8,128)(2,1)S(1)} %bitcast.65), kind=kOutput, calls=%fused_computation.21 | convolution fusion | flops 1140850688 | bytes 8913408 | tf_op jit(solution)/shard_map/kbs,ksf->kbf/dot_general | solution.py:84
  530.7 39.9 %copy.10 = bf16[4,2,4096,128]{3,0,2,1:T(4,128)(2,1)} copy(bf16[4,2,4096,128]{3,2,1,0:T(8,128)(2,1)S(1)} %bitcast.66) | data formatting | bytes 16777216 | tf_op jit(solution)/shard_map/squeeze | solution.py:68
  570.6 63.2 %fusion.27 = f32[4,256,128]{1,2,0:T(8,128)S(1)} fusion(f32[4,256,128]{1,2,0:T(8,128)S(1)} %fusion.11, bf16[4,2,4096,128]{3,2,1,0:T(8,128)(2,1)S(1)} %bitcast.67, s32[4]{0:T(128)S(1)} %dynamic_slice.3, s32[256,4096]{1,0:T(8,128)S(1)} %copy-done.1), kind=kOutput, calls=%fused_computation.46 | convolution fusion | flops 1141112832 | bytes 9437696 | tf_op jit(solution)/shard_map/kbs,ksf->kbf/dot_general | solution.py:83
  633.9 63.7 %fusion.31 = f32[4,256]{1,0:T(4,128)S(1)} fusion(f32[4,256,128]{1,2,0:T(8,128)S(1)} %fusion.27, f32[4,256,128]{1,2,0:T(8,128)S(1)} %fusion.10, bf16[4,2,4096,128]{3,2,1,0:T(8,128)(2,1)S(1)} %bitcast.68, s32[4]{0:T(128)S(1)} %dynamic_slice.3, s32[256,4096]{1,0:T(8,128)S(1)} %copy-done.1), kind=kOutput, calls=%fused_computation.50 | convolution fusion | flops 1141373952 | bytes 9441792 | tf_op jit(solution)/shard_map/kbs,ksf->kbf/dot_general | solution.py:86
  697.6 0.6 broadcast_multiply_fusion
  698.2 37.5 %gather_fusion = bf16[4096,4,2,128]{3,1,2,0:T(4,128)(2,1)} fusion(bf16[4,2,4096,128]{3,0,2,1:T(4,128)(2,1)} %copy.10, s32[4096]{0:T(1024)S(1)} %fusion.45), kind=kCustom, calls=%fused_computation | custom fusion | bytes 16793600 | tf_op jit(solution)/shard_map/jit(_take)/gather | solution.py:70
  735.6 7.9 %copy.12 = bf16[4,2,4096,128]{3,2,1,0:T(8,128)(2,1)} copy(bf16[4,2,4096,128]{3,0,1,2:T(4,128)(2,1)} %bitcast.61) | data formatting | bytes 16777216 | tf_op jit(solution)/shard_map/jit(_take)/gather | solution.py:70
  743.5 1.0 slice_select_fusion
  744.6 4.7 bitcast_select_fusion
  749.3 8.1 %fusion.85 = f32[4,128,8192]{2,1,0:T(8,128)} fusion(bf16[4,128,128]{2,1,0:T(8,128)(2,1)S(1)} %bitcast.71, bf16[4,8192,128]{2,1,0:T(8,128)(2,1)S(1)} %bitcast_select_fusion), kind=kOutput, calls=%fused_computation.128 | convolution fusion | flops 1073741824 | bytes 25296896 | tf_op jit(solution)/shard_map/kaf,kbf->kab/dot_general | solution.py:73
  757.4 6.5 fusion.20
  763.9 3.9 pad_maximum_fusion
  (8 shorter events, 0.1 us)
Async XLA Ops:
  109.0 27.6 %copy-start.2 = (s32[4096]{0:T(1024)S(1)}, s32[4096]{0:T(1024)}, u32[]{:S(2)}) copy-start(s32[4096]{0:T(1024)} %param.5) | copy-start | bytes 49156
  109.0 120.3 %all-to-all-start = ((bf16[128,4,2,32,128]{4,3,2,1,0:T(8,128)(2,1)}), bf16[128,4,2,32,128]{4,3,2,1,0:T(8,128)(2,1)}, u32[]{:S(2)}, u32[]{:S(2)}) async-start(bf16[128,4,2,32,128]{4,3,2,1,0:T(8,128)(2,1)} %bitcast.63), calls=%async_computation | async-start | bytes 16777216 | tf_op jit(solution)/shard_map/all_to_all | solution.py:67
  121.0 274.1 %all-gather.2.cloned.1.call-start = ((), (), s32[]{:S(2)}) async-start(), calls=%async_computation.1 | async-start | bytes 4227072 | tf_op jit(solution)/shard_map/all_gather | solution.py:77
  400.8 67.0 %copy-start = (bf16[1,4,2,128,32,128]{5,4,3,2,1,0:T(8,128)(2,1)S(1)}, bf16[1,4,2,128,32,128]{5,4,3,2,1,0:T(8,128)(2,1)}, u32[]{:S(2)}) copy-start(bf16[1,4,2,128,32,128]{5,4,3,2,1,0:T(8,128)(2,1)} %copy.9) | copy-start | bytes 25165828
  400.8 67.0 %copy-start.1 = (s32[256,4096]{1,0:T(8,128)S(1)}, s32[256,4096]{1,0:T(8,128)}, u32[]{:S(2)}) copy-start(s32[256,4096]{1,0:T(8,128)} %copy.13) | copy-start | bytes 12582916
Sparse Core Ops, SparseCore 0:
  136.7 258.3 all-gather.1
where the time goes:
time: 784 us; the launch traced here: 775 us
  matrix products  308 us (39%)
  waiting for transfers between devices  250 us (32%)
  local copies, waits for them, and re-layouts  140 us (18%)
  other arithmetic  35.9 us (5%)
  starting transfers between devices  27.5 us (4%)
  between operations  14.4 us (2%)
    all_gather x1, waiting for transfers between devices, per_device(): steer_all = lax.all_gather(steer, ('inp', 'grp'), axis=1, tiled=True)  157 us
    all_to_all x1, waiting for transfers between devices, per_device(): lax.all_to_all(outgoing, ('inp', 'grp'), split_axis=0, concat_axis=3, til...  92.6 us
    dot_general x1, matrix products, per_device(): jnp.einsum('kbs,ksf->kbf', wcos, real_in, preferred_element_type=jnp.floa...  67 us
    dot_general x1, matrix products, per_device(): jnp.einsum('kbs,ksf->kbf', wsin, real_in, preferred_element_type=jnp.floa...  63.7 us
    dot_general x1, matrix products, per_device(): jnp.einsum('kbs,ksf->kbf', wsin, imag_in, preferred_element_type=jnp.floa...  63.2 us
    dot_general x1, matrix products, per_device(): jnp.einsum('kbs,ksf->kbf', wcos, imag_in, preferred_element_type=jnp.floa...  62.9 us
    gather x2, local copies, waits for them, and re-layouts, per_device(): permuted = jnp.take(chan_data, slot_map, axis=2)  45.3 us
    dot_general x1, matrix products, per_device(): jnp.einsum('rcn,sfn->crsf', table, filtered, preferred_element_type=jnp.f...  42.6 us
  transfers between devices with their start and end apart: 2, of which 2 were waited for; matrix products, arithmetic and copies ran while one was open for 1% of the time, Pallas kernels for 0%

commit v1 on v0

v1 whole, which is shorter than its diff:
```python
import functools
import math

import jax
import jax.numpy as jnp
import numpy as np
from jax import lax
from jax.experimental import pallas as pl
from jax.experimental.pallas import tpu as pltpu
from jax.sharding import PartitionSpec as P

MESH = pl.DeviceIdType.MESH
NS = 4096
NFFT = 2048
BEAMS = 256
TAPS = 4
CH_GRP = 128
ROWS = 64
FRAMES = 128
N_INP = 32
N_GRP = 4
COUNT = N_INP * N_GRP
CH_DEV = CH_GRP * N_GRP // COUNT
NS_DEV = NS // COUNT
SAMPLES = (FRAMES + TAPS - 1) * NFFT
HALVES = 2
NS_HALF = NS_DEV // HALVES
PARTS = 2 * CH_DEV
BLOCK = NS_HALF * PARTS
MIB = 2**20
F32 = jnp.float32
BF16 = jnp.bfloat16


def prototype():
    pos = np.arange(TAPS * NFFT, dtype=np.float64) + 0.5
    arg = pos / NFFT - TAPS / 2.0
    window = 0.5 - 0.5 * np.cos(2.0 * math.pi * pos / (TAPS * NFFT))
    return (np.sinc(arg) * window).reshape(TAPS, NFFT).astype(np.float32)


def dft_table():
    sub = NFFT // 2 // N_GRP
    order = np.arange(CH_GRP * N_GRP)
    device, inner = order // CH_DEV, order % CH_DEV
    chans = device % N_GRP * sub + (sub - CH_GRP) // 2 + device // N_GRP * CH_DEV + inner
    angle = 2.0 * math.pi * (chans[:, None] * np.arange(NFFT)[None, :] % NFFT) / NFFT
    both = np.stack([np.cos(angle), -np.sin(angle)], axis=1) / math.sqrt(NFFT)
    return both.astype(np.float32).astype(jnp.bfloat16).reshape(COUNT * PARTS, NFFT)


def orbits():
    seen, out = set(), []
    for a in range(4):
        for b in range(4):
            for c in range(4):
                if (a, b, c) == (0, 0, 0) or (a, b, c) in seen:
                    continue
                orbit = []
                for turn in ((a, b, c), (b, c, a), (c, a, b)):
                    for sign in (1, -1):
                        item = tuple(sign * v % 4 for v in turn)
                        if item not in orbit:
                            orbit.append(item)
                seen.update(orbit)
                out.append(orbit)
    return out


def neighbour(dx, dy, dz, dc):
    inp, grp = lax.axis_index("inp"), lax.axis_index("grp")
    x = (inp // 8 + dx) % 4
    y = (grp // 2 * 2 + inp // 4 % 2 + dy) % 4
    z = (inp % 4 + dz) % 4
    core = (grp % 2 + dc) % 2
    return x * 8 + y % 2 * 4 + z, y // 2 * 2 + core


def for_peers(body):
    for orbit in orbits():
        a, b, c = orbit[0]
        size = len(orbit)
        pairs = 2 if size in (6, 2) else 1

        def step(i, carry, a=a, b=b, c=c, size=size, pairs=pairs):
            core, item = i // size, i % size
            turn, sign = item // pairs, 1 - 2 * (item % pairs)
            dx = jnp.where(turn == 0, a, jnp.where(turn == 1, b, c))
            dy = jnp.where(turn == 0, b, jnp.where(turn == 1, c, a))
            dz = jnp.where(turn == 0, c, jnp.where(turn == 1, a, b))
            body(*neighbour(dx * sign + 4, dy * sign + 4, dz * sign + 4, core))
            return carry

        lax.fori_loop(0, 2 * size, step, 0)
    body(*neighbour(0, 0, 0, 1))


def sine(m):
    u = m.astype(F32) * (1.0 / 64.0)
    v = u * u
    p = 1.5148419e-4 * v - 4.673767e-3
    p = p * v + 7.968967e-2
    p = p * v - 6.4596371e-1
    p = p * v + 1.5707963
    return p * u * (1.0 / math.sqrt(NS))


def weights(phase):
    wcos = sine(jnp.abs((phase & 255) - 128) - 64)
    wsin = sine(jnp.abs(((phase - 64) & 255) - 128) - 64)
    return wcos.astype(BF16), wsin.astype(BF16)


def channel_kernel(
    raw, table, proto, steer, x_ref, power,
    rawb, tab, fb, turn, send, xb, xf, beam, wts, words, packs, pack,
    raw_sem, tab_sem, send_sem, recv_sem, own_sem, x_sem, st_send, st_recv,
):
    inp, grp = lax.axis_index("inp"), lax.axis_index("grp")
    me = inp * N_GRP + grp

    for_peers(lambda i, g: pl.semaphore_signal(
        pltpu.get_barrier_semaphore(), inc=1, device_id=(i, g), device_id_type=MESH))

    cuts = (0, 35, 67, 99, 131)

    def raw_copy(half, part):
        lo, hi = cuts[part] * NFFT, cuts[part + 1] * NFFT
        return pltpu.make_async_copy(
            raw.at[pl.ds(half * NS_HALF, NS_HALF), pl.ds(lo, hi - lo)],
            rawb.at[:, pl.ds(lo, hi - lo)], raw_sem.at[part])

    for part in range(4):
        raw_copy(0, part).start()
    tab_copy = pltpu.make_async_copy(table, tab, tab_sem)
    tab_copy.start()

    word = steer[0:64, :] & 255
    for byte in range(1, 4):
        word = word + (steer[byte * 64:(byte + 1) * 64, :] & 255) * (1 << (8 * byte))
    words[...] = jnp.zeros_like(words)
    words[:, 0:NS_DEV] = word
    lane = lax.broadcasted_iota(jnp.int32, (8, 128), 1) // 16
    for half in range(HALVES):
        total = jnp.zeros((8, 128), jnp.int32)
        for eq in range(8):
            moved = pltpu.roll(words[eq * 8:(eq + 1) * 8, :], (eq - half) * 16 % 128, 1)
            total = jnp.where(lane == eq, moved, total)
        packs[me, pl.ds(half * 8, 8), :] = total

    def filter_part(part):
        def body(it, carry):
            f0 = part * 32 + it // 8 * 16
            for sub in range(2):
                n0 = pl.multiple_of(it % 8 * 256 + sub * 128, 128)
                vals = [
                    rawb[:, pl.ds(pl.multiple_of((f0 + g) * NFFT + n0, 128), 128)].astype(F32)
                    for g in range(16 + TAPS - 1)
                ]
                taps = [proto[t:t + 1, pl.ds(n0, 128)] for t in range(TAPS)]
                for f in range(16):
                    acc = taps[0] * vals[f]
                    for t in range(1, TAPS):
                        acc = acc + taps[t] * vals[f + t]
                    turn[sub, f * NS_HALF:(f + 1) * NS_HALF, :] = acc
                for s in range(NS_HALF):
                    rows = turn[sub, pl.ds(s, 16, stride=NS_HALF), :].astype(BF16)
                    fb[pl.ds(pl.multiple_of(s * FRAMES + f0, 16), 16), pl.ds(n0, 128)] = rows
            return carry

        lax.fori_loop(0, 16, body, 0)

    def transform(half):
        def body(pair, carry):
            cols = fb[pl.ds(pl.multiple_of(pair * 256, 256), 256), :]
            for kt in range(4):
                out = lax.dot_general(
                    tab[kt * 256:(kt + 1) * 256, :], cols,
                    (((1,), (1,)), ((), ())), preferred_element_type=F32)
                first = out[:, :128].reshape(32, PARTS, 128)
                second = out[:, 128:].reshape(32, PARTS, 128)
                both = jnp.concatenate([first, second], axis=1).astype(BF16)
                send[half, kt * 32:(kt + 1) * 32, pl.ds(pl.multiple_of(pair * 16, 16), 16), :] = both
            return carry

        lax.fori_loop(0, NS_HALF // 2, body, 0)

    def spread(half):
        def one(i, g):
            pltpu.make_async_remote_copy(
                src_ref=send.at[half, i * N_GRP + g],
                dst_ref=x_ref.at[me, pl.ds(half * BLOCK, BLOCK)],
                send_sem=send_sem.at[half], recv_sem=recv_sem.at[half],
                device_id=(i, g), device_id_type=MESH).start()

        for_peers(one)
        pltpu.make_async_copy(
            send.at[half, me], x_ref.at[me, pl.ds(half * BLOCK, BLOCK)], own_sem.at[half]).start()

    def steer_copies(stage):
        if stage == 0:
            src = packs.at[pl.ds(me, 1)]
            to = [(inp, (grp + k) % 4) for k in range(1, 4)]
        elif stage == 1:
            src = packs.at[pl.ds(inp * 4, 4)]
            to = [(inp // 4 * 4 + (inp + k) % 4, grp) for k in range(1, 4)]
        else:
            src = packs.at[pl.ds(inp // 4 * 16, 16)]
            to = [((inp // 4 + k) % 8 * 4 + inp % 4, grp) for k in range(1, 8)]
        return [
            pltpu.make_async_remote_copy(
                src_ref=src, dst_ref=src, send_sem=st_send.at[stage], recv_sem=st_recv.at[stage],
                device_id=d, device_id_type=MESH) for d in to
        ]

    def steer_start(stage):
        for copy in steer_copies(stage):
            copy.start()

    def steer_wait(stage):
        size = (3, 12, 112)[stage]
        done = pltpu.make_async_remote_copy(
            src_ref=packs.at[pl.ds(0, size)], dst_ref=packs.at[pl.ds(0, size)],
            send_sem=st_send.at[stage], recv_sem=st_recv.at[stage],
            device_id=(inp, (grp + 1) % 4), device_id_type=MESH)
        done.wait_send()
        done.wait_recv()

    for part in range(4):
        raw_copy(0, part).wait()
        filter_part(part)
    for part in range(4):
        raw_copy(1, part).start()
    pl.semaphore_wait(pltpu.get_barrier_semaphore(), COUNT - 1)
    steer_start(0)
    tab_copy.wait()
    transform(0)
    spread(0)
    steer_wait(0)
    steer_start(1)
    for part in range(4):
        raw_copy(1, part).wait()
        filter_part(part)
    steer_wait(1)
    steer_start(2)
    transform(1)
    spread(1)
    steer_wait(2)

    def weigh(it, carry):
        half, tile = it // 16, it % 16
        base = tile * 8
        for eq in range(8):
            total = jnp.zeros((8, 128), jnp.int32)
            for dd in range(8):
                block = packs[base + dd, pl.ds(pl.multiple_of(half * 8, 8), 8), :]
                total = jnp.where(lane == dd, pltpu.roll(block, (dd - eq) * 16 % 128, 1), total)
            pack[eq * 8:(eq + 1) * 8, :] = total
        col = pl.multiple_of(tile * 128, 128)
        for byte in range(4):
            index = (pack[...] >> (8 * byte)) & 255
            for j in range(CH_DEV):
                wcos, wsin = weights(index * (inp * CH_DEV + ((NFFT // 2 // N_GRP - CH_GRP) // 2 + j)))
                wts[j, half, byte * 64:(byte + 1) * 64, pl.ds(col, 128)] = wcos
                wts[j, half, byte * 64:(byte + 1) * 64, pl.ds(col + 2048, 128)] = wsin
        return carry

    lax.fori_loop(0, 16 * HALVES, weigh, 0)
    beam[...] = jnp.zeros_like(beam)

    for half in range(HALVES):
        done = pltpu.make_async_remote_copy(
            src_ref=send.at[half, pl.ds(0, COUNT - 1)],
            dst_ref=x_ref.at[pl.ds(0, COUNT - 1), pl.ds(half * BLOCK, BLOCK)],
            send_sem=send_sem.at[half], recv_sem=recv_sem.at[half],
            device_id=(inp, (grp + 1) % 4), device_id_type=MESH)
        done.wait_send()
        done.wait_recv()
        pltpu.make_async_copy(
            send.at[half, me], x_ref.at[me, pl.ds(half * BLOCK, BLOCK)], own_sem.at[half]).wait()
        fetch = pltpu.make_async_copy(x_ref.at[:, pl.ds(half * BLOCK, BLOCK)], xb, x_sem)
        fetch.start()
        fetch.wait()

        def add(sb, carry, half=half):
            xf[...] = xb[pl.ds(sb * 16, 16)].astype(F32).reshape(16 * BLOCK, 128)
            for j in range(CH_DEV):
                re = xf[pl.ds(2 * j, 256, stride=PARTS), :]
                im = xf[pl.ds(2 * j + 1, 256, stride=PARTS), :]
                ab = jnp.concatenate([re, im], axis=1).astype(BF16)
                ba = jnp.concatenate([im, -re], axis=1).astype(BF16)
                col = pl.multiple_of(sb * 256, 256)
                beam[j] += jnp.dot(
                    wts[j, half, :, pl.ds(col, 256)], ab, preferred_element_type=F32
                ) + jnp.dot(
                    wts[j, half, :, pl.ds(col + 2048, 256)], ba, preferred_element_type=F32)
            return carry

        lax.fori_loop(0, 8, add, 0)

    for j in range(CH_DEV):
        value = beam[j]
        square = value * value
        folded = (square[:, :128] + square[:, 128:]).T
        power[j:j + 1, :] = jnp.sum(folded, axis=0, keepdims=True) * (1.0 / FRAMES)


def gram_kernel(slots, x_ref, out, xb, xf, yf, left, sems):
    step = pl.program_id(0)

    def gather(first, count):
        def body(i, carry):
            for k in range(8):
                q = i * 8 + k
                row = pl.multiple_of(slots[first + q] * PARTS, PARTS)
                yf[pl.ds(pl.multiple_of(q * PARTS, PARTS), PARTS), :] = xf[pl.ds(row, PARTS), :]
            return carry

        lax.fori_loop(0, count // 8, body, 0)

    @pl.when(step == 0)
    def _():
        copies = [
            pltpu.make_async_copy(
                x_ref.at[pl.ds(k * 16, 16)], xb.at[pl.ds(k * 16, 16)], sems.at[k]) for k in range(8)
        ]
        for copy in copies:
            copy.start()
        for k, copy in enumerate(copies):
            copy.wait()

            def widen(i, carry):
                dev = k * 16 + i
                rows = pl.ds(pl.multiple_of(dev * 256, 256), 256)
                xf[rows, :] = xb[dev].astype(F32)
                return carry

            lax.fori_loop(0, 16, widen, 0)
        gather(0, ROWS)
        for j in range(CH_DEV):
            re = yf[pl.ds(2 * j, ROWS, stride=PARTS), :]
            im = yf[pl.ds(2 * j + 1, ROWS, stride=PARTS), :]
            upper = jnp.concatenate([re, im], axis=1)
            lower = jnp.concatenate([-im, re], axis=1)
            left[j] = jnp.concatenate([upper, lower], axis=0).astype(BF16)

    gather(step * 256, 256)
    for j in range(CH_DEV):
        re = yf[pl.ds(2 * j, 256, stride=PARTS), :]
        im = yf[pl.ds(2 * j + 1, 256, stride=PARTS), :]
        right = jnp.concatenate([re, im], axis=1).astype(BF16)
        prod = lax.dot_general(
            left[j], right, (((1,), (1,)), ((), ())), preferred_element_type=F32)
        prod = prod * (1.0 / FRAMES)
        out[0, j * ROWS:(j + 1) * ROWS, :] = prod[:ROWS]
        out[1, j * ROWS:(j + 1) * ROWS, :] = prod[ROWS:]


def per_device(raw, steer, slot_map):
    anywhere = pl.BlockSpec(memory_space=pl.ANY)
    vmem = pl.BlockSpec(memory_space=pltpu.VMEM)
    dma = pltpu.SemaphoreType.DMA
    spectra, power = pl.pallas_call(
        channel_kernel,
        out_shape=(
            jax.ShapeDtypeStruct((COUNT, HALVES * BLOCK, FRAMES), BF16),
            jax.ShapeDtypeStruct((CH_DEV, BEAMS), F32),
        ),
        in_specs=[anywhere, anywhere, vmem, vmem],
        out_specs=(anywhere, vmem),
        scratch_shapes=[
            pltpu.VMEM((NS_HALF, SAMPLES), BF16),
            pltpu.VMEM((COUNT * PARTS, NFFT), BF16),
            pltpu.VMEM((NS_HALF * FRAMES, NFFT), BF16),
            pltpu.VMEM((2, 16 * NS_HALF, 128), F32),
            pltpu.VMEM((HALVES, COUNT, BLOCK, FRAMES), BF16),
            pltpu.VMEM((COUNT, BLOCK, FRAMES), BF16),
            pltpu.VMEM((16 * BLOCK, FRAMES), F32),
            pltpu.VMEM((CH_DEV, BEAMS, 2 * FRAMES), F32),
            pltpu.VMEM((CH_DEV, HALVES, BEAMS, NS), BF16),
            pltpu.VMEM((64, 128), jnp.int32),
            pltpu.VMEM((COUNT, 16, 128), jnp.int32),
            pltpu.VMEM((64, 128), jnp.int32),
            dma((4,)), dma, dma((HALVES,)), dma((HALVES,)), dma((HALVES,)), dma,
            dma((3,)), dma((3,)),
        ],
        compiler_params=pltpu.CompilerParams(
            collective_id=0, has_side_effects=True, vmem_limit_bytes=62 * MIB),
        name="channelize",
    )(raw, jnp.asarray(dft_table()), jnp.asarray(prototype()), steer)
    visibility = pl.pallas_call(
        gram_kernel,
        out_shape=jax.ShapeDtypeStruct((2, CH_DEV * ROWS, NS), F32),
        grid=(NS // 256,),
        in_specs=[pl.BlockSpec(memory_space=pltpu.SMEM), anywhere],
        out_specs=pl.BlockSpec((2, CH_DEV * ROWS, 256), lambda i: (0, 0, i)),
        scratch_shapes=[
            pltpu.VMEM((COUNT, HALVES * BLOCK, FRAMES), BF16),
            pltpu.VMEM((NS * PARTS, FRAMES), F32),
            pltpu.VMEM((256 * PARTS, FRAMES), F32),
            pltpu.VMEM((CH_DEV, 2 * ROWS, 2 * FRAMES), BF16),
            dma((8,)),
        ],
        compiler_params=pltpu.CompilerParams(vmem_limit_bytes=48 * MIB),
        name="gram",
    )(slot_map, spectra)
    return visibility, power


def solution(mesh):
    in_specs = (P(("inp", "grp"), None), P(None, ("inp", "grp")), P())
    out_specs = (P(None, ("inp", "grp"), None), P(("inp", "grp"), None))
    return jax.shard_map(
        per_device, mesh=mesh, in_specs=in_specs, out_specs=out_specs, check_vma=False
    )
```

time: 784 us -> 177 us (0.23); the launches traced: 775 us -> 176 us
  matrix products: 308 us -> 0 us
  waiting for transfers between devices: 250 us -> 0 us
  Pallas kernels: 0 us -> 173 us
  local copies, waits for them, and re-layouts: 140 us -> 2.12 us
  other arithmetic: 35.9 us -> 0 us
  starting transfers between devices: 27.5 us -> 0 us
  between operations: 14.4 us -> 0.67 us
    dot_general x6 -> x0, matrix products: 308 us -> none  [the longest x1 67 us: per_device(): jnp.einsum('kbs,ksf->kbf', wcos, real_in, preferred_element_type=jnp.floa...]
    pallas_call x0 -> x2, Pallas kernels: none -> 173 us  [the longest x1 154 us: per_device(): pl.pallas_call(channel_kernel, out_shape=(jax.ShapeDtypeStruct((COUNT, HA...]
    all_gather x1 -> x0, waiting for transfers between devices: 157 us -> none  [per_device(): steer_all = lax.all_gather(steer, ('inp', 'grp'), axis=1, tiled=True)]
    all_to_all x1 -> x0, waiting for transfers between devices: 92.6 us -> none  [per_device(): lax.all_to_all(outgoing, ('inp', 'grp'), split_axis=0, concat_axis=3, til...]
    gather x2 -> x0, local copies, waits for them, and re-layouts: 45.3 us -> none  [per_device(): permuted = jnp.take(chan_data, slot_map, axis=2)]
    squeeze x1 -> x0, local copies, waits for them, and re-layouts: 39.9 us -> none  [per_device(): chan_data = arrived[0]]
    reshape x1 -> x0, local copies, waits for them, and re-layouts: 25.2 us -> none  [per_device(): view = raw.reshape(ns_dev, frames + TAPS - 1, NFFT)]
    another operation x2 -> x0, other arithmetic: 22.9 us -> none
  transfers between devices with their start and end apart: 2 -> 0, of which waited for: 2 -> 0; matrix products, arithmetic and copies ran while one was open for 1% -> 0% of each run, Pallas kernels for 0% -> 0%
where the time goes in v1:
time: 177 us; the launch traced here: 176 us
  Pallas kernels  173 us (98%)
  local copies, waits for them, and re-layouts  2.12 us (1%)
    pallas_call x1, Pallas kernels, per_device(): pl.pallas_call(channel_kernel, out_shape=(jax.ShapeDtypeStruct((COUNT, HA...  154 us
    pallas_call x1, Pallas kernels, per_device(): pl.pallas_call(gram_kernel, out_shape=jax.ShapeDtypeStruct((2, CH_DEV * R...  18.7 us

profile of v1, /device:TPU:1, one launch (start us, length us, event | category | flops | bytes accessed | tf_op | source)
XLA Modules:
  0.0 175.9 jit_solution(15177052921911181996)
XLA Ops:
  0.6 1.5 copy.7.steer
  2.1 0.0 copy-start
  2.1 154.3 %channelize.1 = (bf16[128,256,128]{2,1,0:T(8,128)(2,1)}, f32[4,256]{1,0:T(4,128)}) custom-call(bf16[32,268288]{1,0:T(8,128)(2,1)} %raw.1, bf16[1024,2048]{1,0:T(8,128)(2,1)} %constant.4.clone.table, f32[4,2048]{1,0:T(4,128)} %constant.5.clone.proto, s32[256,32]{1,0:T(8,128)} %copy.7.steer), custom_call_target="tpu_custom_call" | custom-call | tf_op jit(solution)/shard_map/channelize/pallas_call | solution.py:363
  156.5 0.0 copy-done
  156.5 0.0 copy-start.1
  156.5 18.7 %gram.1 = f32[2,256,4096]{2,1,0:T(8,128)} custom-call(s32[4096]{0:T(1024)S(1)} %copy-done, bf16[128,256,128]{2,1,0:T(8,128)(2,1)} %get-tuple-element.4.x_ref), custom_call_target="tpu_custom_call" | custom-call | tf_op jit(solution)/shard_map/gram/pallas_call | solution.py:391
  175.3 0.0 copy-done.1
  175.3 0.6 copy.9
Async XLA Ops:
  2.1 154.3 %copy-start = (s32[4096]{0:T(1024)S(1)}, s32[4096]{0:T(1024)}, u32[]{:S(2)}) copy-start(s32[4096]{0:T(1024)} %slots.1) | copy-start | bytes 49156
  156.5 18.8 %copy-start.1 = (f32[4,256]{1,0:T(4,128)S(1)}, f32[4,256]{1,0:T(4,128)}, u32[]{:S(2)}) copy-start(f32[4,256]{1,0:T(4,128)} %get-tuple-element.9) | copy-start | bytes 12292

commit v2 on v1

v2 whole, which is shorter than its diff:
```python
import functools
import math

import jax
import jax.numpy as jnp
import numpy as np
from jax import lax
from jax.experimental import pallas as pl
from jax.experimental.pallas import tpu as pltpu
from jax.sharding import PartitionSpec as P

MESH = pl.DeviceIdType.MESH
NS = 4096
NFFT = 2048
BEAMS = 256
TAPS = 4
CH_GRP = 128
ROWS = 64
FRAMES = 128
N_INP = 32
N_GRP = 4
COUNT = N_INP * N_GRP
CH_DEV = CH_GRP * N_GRP // COUNT
NS_DEV = NS // COUNT
SAMPLES = (FRAMES + TAPS - 1) * NFFT
CHUNKS = 4
NS_CHUNK = NS_DEV // CHUNKS
PARTS = 2 * CH_DEV
BLOCK = NS_CHUNK * PARTS
KEYS = COUNT * NS_CHUNK
MIB = 2**20
F32 = jnp.float32
BF16 = jnp.bfloat16


def prototype():
    pos = np.arange(TAPS * NFFT, dtype=np.float64) + 0.5
    arg = pos / NFFT - TAPS / 2.0
    window = 0.5 - 0.5 * np.cos(2.0 * math.pi * pos / (TAPS * NFFT))
    return (np.sinc(arg) * window).reshape(TAPS, NFFT).astype(np.float32)


def dft_table():
    sub = NFFT // 2 // N_GRP
    order = np.arange(CH_GRP * N_GRP)
    device, inner = order // CH_DEV, order % CH_DEV
    chans = device % N_GRP * sub + (sub - CH_GRP) // 2 + device // N_GRP * CH_DEV + inner
    angle = 2.0 * math.pi * (chans[:, None] * np.arange(NFFT)[None, :] % NFFT) / NFFT
    both = np.stack([np.cos(angle), -np.sin(angle)], axis=1) / math.sqrt(NFFT)
    return both.astype(np.float32).astype(jnp.bfloat16).reshape(COUNT * PARTS, NFFT)


def orbits():
    seen, out = set(), []
    for a in range(4):
        for b in range(4):
            for c in range(4):
                if (a, b, c) == (0, 0, 0) or (a, b, c) in seen:
                    continue
                orbit = []
                for sign in (1, -1):
                    for turn in ((a, b, c), (b, c, a), (c, a, b)):
                        item = tuple(sign * v % 4 for v in turn)
                        if item not in orbit:
                            orbit.append(item)
                seen.update(orbit)
                out.append(orbit)
    return out


def neighbour(dx, dy, dz, dc):
    inp, grp = lax.axis_index("inp"), lax.axis_index("grp")
    x = (inp // 8 + dx) % 4
    y = (grp // 2 * 2 + inp // 4 % 2 + dy) % 4
    z = (inp % 4 + dz) % 4
    core = (grp % 2 + dc) % 2
    return x * 8 + y % 2 * 4 + z, y // 2 * 2 + core


def for_peers(body):
    way = 1 - 2 * (lax.axis_index("grp") % 2)
    for orbit in orbits():
        a, b, c = orbit[0]
        size = len(orbit)
        turns = 3 if size % 3 == 0 else 1

        def step(i, carry, a=a, b=b, c=c, size=size, turns=turns):
            core, item = i // size, i % size
            turn, sign = item % turns, (1 - 2 * (item // turns)) * way
            dx = jnp.where(turn == 0, a, jnp.where(turn == 1, b, c))
            dy = jnp.where(turn == 0, b, jnp.where(turn == 1, c, a))
            dz = jnp.where(turn == 0, c, jnp.where(turn == 1, a, b))
            body(*neighbour(dx * sign + 4, dy * sign + 4, dz * sign + 4, core))
            return carry

        lax.fori_loop(0, 2 * size, step, 0)
    body(*neighbour(0, 0, 0, 1))


def sine(m):
    u = m.astype(F32) * (1.0 / 64.0)
    v = u * u
    p = 1.5148419e-4 * v - 4.673767e-3
    p = p * v + 7.968967e-2
    p = p * v - 6.4596371e-1
    p = p * v + 1.5707963
    return p * u * (1.0 / math.sqrt(NS))


def weights(phase):
    wcos = sine(jnp.abs((phase & 255) - 128) - 64)
    wsin = sine(jnp.abs(((phase - 64) & 255) - 128) - 64)
    return wcos.astype(BF16), wsin.astype(BF16)


def channel_kernel(
    raw, table, proto, steer, x_ref, power,
    rawb, tab, fb, turn, send, xv, xf, beam, wts, words, owns, packs, pack,
    raw_sem, tab_sem, send_sem, recv_sem, own_sem, x_sem, st_send, st_recv,
):
    inp, grp = lax.axis_index("inp"), lax.axis_index("grp")
    me = inp * N_GRP + grp

    x, ylo, z = inp // 8, inp // 4 % 2, inp % 4
    core = grp % 2
    mine = pl.ds(pl.multiple_of(core * 8, 8), 8)
    cuts = (0, 35, 67, 99, 131)

    def raw_copy(half, part):
        lo, hi = cuts[part] * NFFT, cuts[part + 1] * NFFT
        return pltpu.make_async_copy(
            raw.at[pl.ds(half * 16, 16), pl.ds(lo, hi - lo)],
            rawb.at[:, pl.ds(lo, hi - lo)], raw_sem.at[part])

    for part in range(4):
        raw_copy(0, part).start()
    tab_copy = pltpu.make_async_copy(table, tab, tab_sem)
    tab_copy.start()

    for_peers(lambda i, g: pl.semaphore_signal(
        pltpu.get_barrier_semaphore(), inc=1, device_id=(i, g), device_id_type=MESH))

    def pack_steer():
        low, high = steer[:, 0:128] & 255, steer[:, 128:256] & 255
        words[...] = jnp.zeros_like(words)
        words[0:NS_DEV, :] = (
            low + (pltpu.roll(low, 64, 1) << 8) + (high << 16) + (pltpu.roll(high, 64, 1) << 24))
        words[...] = words[...].T
        lane = lax.broadcasted_iota(jnp.int32, (4, 128), 1) // 8
        for chunk in range(CHUNKS):
            total = jnp.zeros((4, 128), jnp.int32)
            for eq in range(16):
                moved = pltpu.roll(words[eq * 4:(eq + 1) * 4, :], (eq - chunk) * 8 % 128, 1)
                total = jnp.where(lane == eq, moved, total)
            owns[chunk * 4:(chunk + 1) * 4, :] = total
        packs[x, ylo, z, grp, mine, :] = owns[mine, :]

    def filter_part(chunk, part):
        row = chunk % 2 * NS_CHUNK

        def body(it, carry):
            f0 = part * 32 + it // 8 * 16
            for sub in range(2):
                n0 = pl.multiple_of(it % 8 * 256 + sub * 128, 128)
                vals = [
                    rawb[:, pl.ds(pl.multiple_of((f0 + g) * NFFT + n0, 128), 128)]
                    .astype(F32)[row:row + NS_CHUNK]
                    for g in range(16 + TAPS - 1)
                ]
                taps = [proto[t:t + 1, pl.ds(n0, 128)] for t in range(TAPS)]
                for f in range(16):
                    acc = taps[0] * vals[f]
                    for t in range(1, TAPS):
                        acc = acc + taps[t] * vals[f + t]
                    turn[sub, f * NS_CHUNK:(f + 1) * NS_CHUNK, :] = acc
                for s in range(NS_CHUNK):
                    rows = turn[sub, pl.ds(s, 16, stride=NS_CHUNK), :].astype(BF16)
                    fb[pl.ds(pl.multiple_of(s * FRAMES + f0, 16), 16), pl.ds(n0, 128)] = rows
            return carry

        lax.fori_loop(0, 16, body, 0)

    def transform(chunk):
        def body(pair, carry):
            cols = fb[pl.ds(pl.multiple_of(pair * 256, 256), 256), :]
            for kt in range(4):
                out = lax.dot_general(
                    tab[kt * 256:(kt + 1) * 256, :], cols,
                    (((1,), (1,)), ((), ())), preferred_element_type=F32)
                first = out[:, :128].reshape(32, PARTS, 128)
                second = out[:, 128:].reshape(32, PARTS, 128)
                both = jnp.concatenate([first, second], axis=1).astype(BF16)
                send[chunk, kt * 32:(kt + 1) * 32, pl.ds(pl.multiple_of(pair * 16, 16), 16), :] = both
            return carry

        lax.fori_loop(0, NS_CHUNK // 2, body, 0)

    def own_copy(chunk):
        return pltpu.make_async_copy(
            send.at[chunk, me], xv.at[me, pl.ds(chunk * BLOCK, BLOCK)], own_sem.at[chunk])

    def spread(chunk):
        def one(i, g):
            pltpu.make_async_remote_copy(
                src_ref=send.at[chunk, i * N_GRP + g],
                dst_ref=xv.at[me, pl.ds(chunk * BLOCK, BLOCK)],
                send_sem=send_sem.at[chunk], recv_sem=recv_sem.at[chunk],
                device_id=(i, g), device_id_type=MESH).start()

        for_peers(one)
        own_copy(chunk).start()

    chip = pl.ds(grp // 2 * 2, 2)
    every = pl.ds(0, 4)
    near = pl.ds(0, 2)

    def steer_send(stage, src, offsets, dst=None):
        for off in offsets:
            pltpu.make_async_remote_copy(
                src_ref=src, dst_ref=src if dst is None else dst, send_sem=st_send.at[stage], recv_sem=st_recv.at[stage],
                device_id=neighbour(*off), device_id_type=MESH).start()

    along = [[tuple(k if axis == d else 0 for d in range(4)) for k in (1, 2, 3)] for axis in range(3)]

    def steer_start(stage):
        if stage == 0:
            other = pl.ds(pl.multiple_of((1 - core) * 8, 8), 8)
            steer_send(0, owns.at[other], [(0, 0, 0, 1)], packs.at[x, ylo, z, grp, other])
        elif stage == 4:
            steer_send(4, packs.at[every, near, every, every, mine], [(0, 0, 0, 1)])
        else:
            first = (packs.at[x, ylo, z, chip, mine], packs.at[x, near, z, every, mine],
                     packs.at[x, near, every, every, mine])[stage - 1]
            second = (packs.at[x, ylo, z, chip, mine], packs.at[every, ylo, z, chip, mine],
                      packs.at[every, near, z, every, mine])[stage - 1]

            @pl.when(core == 0)
            def _():
                steer_send(stage, first, along[(1, 2, 0)[stage - 1]])

            @pl.when(core == 1)
            def _():
                steer_send(stage, second, along[stage - 1])

    def steer_wait(stage):
        span = (
            packs.at[0, 0, 0, 0, mine], packs.at[0, 0, 0, pl.ds(0, 3)],
            packs.at[0, near, pl.ds(0, 3), every, mine],
            packs.at[pl.ds(0, 3), near, every, every, mine],
            packs.at[every, near, every, every, mine])[stage]
        done = pltpu.make_async_remote_copy(
            src_ref=span, dst_ref=span, send_sem=st_send.at[stage], recv_sem=st_recv.at[stage],
            device_id=neighbour(0, 0, 0, 1), device_id_type=MESH)
        done.wait_send()
        done.wait_recv()

    pack_steer()
    for chunk in range(CHUNKS):
        for part in range(4):
            if chunk % 2 == 0:
                raw_copy(chunk // 2, part).wait()
            filter_part(chunk, part)
            if chunk == 0:
                if part == 1:
                    pl.semaphore_wait(pltpu.get_barrier_semaphore(), COUNT - 1)
                elif part > 1:
                    steer_wait(part - 2)
                if part > 0:
                    steer_start(part - 1)
        if chunk == 1:
            for part in range(4):
                raw_copy(1, part).start()
        if chunk == 0:
            tab_copy.wait()
        transform(chunk)
        if chunk == 0:
            steer_wait(2)
            steer_start(3)
        spread(chunk)
        if chunk == 1:
            steer_wait(3)
            steer_start(4)
    steer_wait(4)

    lane = lax.broadcasted_iota(jnp.int32, (8, 128), 1) // 8

    def weigh(it, carry):
        two, tile = it // 8, it % 8
        for eq in range(16):
            total = jnp.zeros((8, 128), jnp.int32)
            for dd in range(16):
                block = packs[tile // 2, tile % 2, dd // 4, dd % 4, pl.ds(pl.multiple_of(two * 8, 8), 8), :]
                total = jnp.where(lane == dd, pltpu.roll(block, (dd - eq) * 8 % 128, 1), total)
            pack[0, eq * 4:(eq + 1) * 4, :] = total[0:4]
            pack[1, eq * 4:(eq + 1) * 4, :] = total[4:8]
        col = pl.multiple_of(tile * 128, 128)
        for one in range(2):
            for byte in range(4):
                index = (pack[one] >> (8 * byte)) & 255
                rows = slice(byte * 64, (byte + 1) * 64)
                for j in range(CH_DEV):
                    chan = inp * CH_DEV + ((NFFT // 2 // N_GRP - CH_GRP) // 2 + j)
                    wcos, wsin = weights(index * chan)
                    wts[j, two * 2 + one, rows, pl.ds(col, 128)] = wcos
                    wts[j, two * 2 + one, rows, pl.ds(col + KEYS, 128)] = wsin
        return carry

    lax.fori_loop(0, 16, weigh, 0)
    beam[...] = jnp.zeros_like(beam)

    def keep(chunk):
        rows = pl.ds(chunk * BLOCK, BLOCK)
        return pltpu.make_async_copy(xv.at[:, rows], x_ref.at[:, rows], x_sem.at[chunk])

    for chunk in range(CHUNKS):
        done = pltpu.make_async_remote_copy(
            src_ref=send.at[chunk, pl.ds(0, COUNT - 1)],
            dst_ref=xv.at[pl.ds(0, COUNT - 1), pl.ds(chunk * BLOCK, BLOCK)],
            send_sem=send_sem.at[chunk], recv_sem=recv_sem.at[chunk],
            device_id=(inp, (grp + 1) % 4), device_id_type=MESH)
        done.wait_send()
        done.wait_recv()
        own_copy(chunk).wait()
        keep(chunk).start()

        def add(sb, carry, chunk=chunk):
            block = xv[pl.ds(sb * 32, 32), chunk * BLOCK:(chunk + 1) * BLOCK, :]
            xf[...] = block.astype(F32).reshape(32 * BLOCK, 128)
            for j in range(CH_DEV):
                re = xf[pl.ds(2 * j, 256, stride=PARTS), :]
                im = xf[pl.ds(2 * j + 1, 256, stride=PARTS), :]
                ab = jnp.concatenate([re, im], axis=1).astype(BF16)
                ba = jnp.concatenate([im, -re], axis=1).astype(BF16)
                col = pl.multiple_of(sb * 256, 256)
                beam[j] += jnp.dot(
                    wts[j, chunk, :, pl.ds(col, 256)], ab, preferred_element_type=F32
                ) + jnp.dot(
                    wts[j, chunk, :, pl.ds(col + KEYS, 256)], ba, preferred_element_type=F32)
            return carry

        lax.fori_loop(0, KEYS // 256, add, 0)

    for j in range(CH_DEV):
        value = beam[j]
        square = value * value
        folded = (square[:, :128] + square[:, 128:]).T
        power[j:j + 1, :] = jnp.sum(folded, axis=0, keepdims=True) * (1.0 / FRAMES)
    for chunk in range(CHUNKS):
        keep(chunk).wait()


def gram_kernel(slots, x_ref, power_in, out, power, xb, xf, yfa, yfb, left, sems):
    step = pl.program_id(0)

    def gather(yf, first, count):
        for q in range(count):
            row = pl.multiple_of(slots[first + q] * PARTS, PARTS)
            yf[q * PARTS:(q + 1) * PARTS, :] = xf[pl.ds(row, PARTS), :]

    def pair(yf, j, count):
        return (yf[pl.ds(2 * j, count, stride=PARTS), :],
                yf[pl.ds(2 * j + 1, count, stride=PARTS), :])

    @pl.when(step == 0)
    def _():
        power[...] = power_in[...]
        copies = [
            pltpu.make_async_copy(
                x_ref.at[pl.ds(k * 16, 16)], xb.at[pl.ds(k * 16, 16)], sems.at[k]) for k in range(8)
        ]
        for copy in copies:
            copy.start()
        for k, copy in enumerate(copies):
            copy.wait()

            def widen(i, carry):
                dev = k * 16 + i
                rows = pl.ds(pl.multiple_of(dev * 256, 256), 256)
                xf[rows, :] = xb[dev].astype(F32)
                return carry

            lax.fori_loop(0, 16, widen, 0)
        gather(yfa, 0, 256)
        for j in range(CH_DEV):
            re, im = pair(yfa, j, ROWS)
            upper = jnp.concatenate([re, im], axis=1)
            lower = jnp.concatenate([-im, re], axis=1)
            left[j] = jnp.concatenate([upper, lower], axis=0).astype(BF16)

    def multiply(yf, col):
        for j in range(CH_DEV):
            right = jnp.concatenate(pair(yf, j, 256), axis=1).astype(BF16)
            prod = lax.dot_general(
                left[j], right, (((1,), (1,)), ((), ())), preferred_element_type=F32)
            prod = prod * (1.0 / FRAMES)
            out[0, j * ROWS:(j + 1) * ROWS, col:col + 256] = prod[:ROWS]
            out[1, j * ROWS:(j + 1) * ROWS, col:col + 256] = prod[ROWS:]

    gather(yfb, step * 512 + 256, 256)
    multiply(yfa, 0)
    gather(yfa, (step + 1) % (NS // 512) * 512, 256)
    multiply(yfb, 256)


def per_device(raw, steer, slot_map):
    anywhere = pl.BlockSpec(memory_space=pl.ANY)
    vmem = pl.BlockSpec(memory_space=pltpu.VMEM)
    dma = pltpu.SemaphoreType.DMA
    spectra, power = pl.pallas_call(
        channel_kernel,
        out_shape=(
            jax.ShapeDtypeStruct((COUNT, CHUNKS * BLOCK, FRAMES), BF16),
            jax.ShapeDtypeStruct((CH_DEV, BEAMS), F32),
        ),
        in_specs=[anywhere, anywhere, vmem, vmem],
        out_specs=(anywhere, vmem),
        scratch_shapes=[
            pltpu.VMEM((16, SAMPLES), BF16),
            pltpu.VMEM((COUNT * PARTS, NFFT), BF16),
            pltpu.VMEM((NS_CHUNK * FRAMES, NFFT), BF16),
            pltpu.VMEM((2, 16 * NS_CHUNK, 128), F32),
            pltpu.VMEM((CHUNKS, COUNT, BLOCK, FRAMES), BF16),
            pltpu.VMEM((COUNT, CHUNKS * BLOCK, FRAMES), BF16),
            pltpu.VMEM((32 * BLOCK, FRAMES), F32),
            pltpu.VMEM((CH_DEV, BEAMS, 2 * FRAMES), F32),
            pltpu.VMEM((CH_DEV, CHUNKS, BEAMS, 2 * KEYS), BF16),
            pltpu.VMEM((128, 128), jnp.int32),
            pltpu.VMEM((16, 128), jnp.int32),
            pltpu.VMEM((4, 2, 4, N_GRP, 16, 128), jnp.int32),
            pltpu.VMEM((2, 64, 128), jnp.int32),
            dma((4,)), dma, dma((CHUNKS,)), dma((CHUNKS,)), dma((CHUNKS,)), dma((CHUNKS,)),
            dma((5,)), dma((5,)),
        ],
        compiler_params=pltpu.CompilerParams(
            collective_id=0, has_side_effects=True, vmem_limit_bytes=62 * MIB),
        name="channelize",
    )(raw, jnp.asarray(dft_table()), jnp.asarray(prototype()), steer.T)
    visibility, power = pl.pallas_call(
        gram_kernel,
        out_shape=(
            jax.ShapeDtypeStruct((2, CH_DEV * ROWS, NS), F32),
            jax.ShapeDtypeStruct((CH_DEV, BEAMS), F32),
        ),
        grid=(NS // 512,),
        in_specs=[pl.BlockSpec(memory_space=pltpu.SMEM), anywhere, vmem],
        out_specs=(pl.BlockSpec((2, CH_DEV * ROWS, 512), lambda i: (0, 0, i)), vmem),
        scratch_shapes=[
            pltpu.VMEM((COUNT, CHUNKS * BLOCK, FRAMES), BF16),
            pltpu.VMEM((NS * PARTS, FRAMES), F32),
            pltpu.VMEM((256 * PARTS, FRAMES), F32),
            pltpu.VMEM((256 * PARTS, FRAMES), F32),
            pltpu.VMEM((CH_DEV, 2 * ROWS, 2 * FRAMES), BF16),
            dma((8,)),
        ],
        compiler_params=pltpu.CompilerParams(vmem_limit_bytes=48 * MIB),
        name="gram",
    )(slot_map, spectra, power)
    return visibility, power


def solution(mesh):
    in_specs = (P(("inp", "grp"), None), P(None, ("inp", "grp")), P())
    out_specs = (P(None, ("inp", "grp"), None), P(("inp", "grp"), None))
    return jax.shard_map(
        per_device, mesh=mesh, in_specs=in_specs, out_specs=out_specs, check_vma=False
    )
```

time: 177 us -> 143 us (0.81)
  Pallas kernels: 173 us -> 142 us
    pallas_call x2, Pallas kernels: 173 us -> 142 us  [the longest x1 128 us: per_device(): pl.pallas_call(channel_kernel, out_shape=(jax.ShapeDtypeStruct((COUNT, CH...]
where the time goes in v2:
time: 143 us
  Pallas kernels  142 us (99%)
    pallas_call x1, Pallas kernels, per_device(): pl.pallas_call(channel_kernel, out_shape=(jax.ShapeDtypeStruct((COUNT, CH...  128 us
    pallas_call x1, Pallas kernels, per_device(): pl.pallas_call(gram_kernel, out_shape=(jax.ShapeDtypeStruct((2, CH_DEV *...  13.6 us

profile of v2, /device:TPU:1, one launch (start us, length us, event | category | flops | bytes accessed | tf_op | source)
XLA Modules:
  0.0 143.1 jit_solution(16175554748851249383)
XLA Ops:
  0.6 0.0 copy-start
  0.6 128.1 %channelize.1 = (bf16[128,256,128]{2,1,0:T(8,128)(2,1)}, f32[4,256]{1,0:T(4,128)}) custom-call(bf16[32,268288]{1,0:T(8,128)(2,1)} %raw.1, bf16[1024,2048]{1,0:T(8,128)(2,1)} %constant.4.clone.table, f32[4,2048]{1,0:T(4,128)} %constant.5.clone.proto, s32[32,256]{1,0:T(8,128)} %bitcast.1), custom_call_target="tpu_custom_call" | custom-call | tf_op jit(solution)/shard_map/channelize/pallas_call | solution.py:409
  128.7 0.0 copy-done
  128.7 0.0 copy-start.1
  128.7 0.7 copy-done.1
  129.4 13.6 %gram.1 = (f32[2,256,4096]{2,1,0:T(8,128)}, f32[4,256]{1,0:T(4,128)}) custom-call(s32[4096]{0:T(1024)S(1)} %copy-done, bf16[128,256,128]{2,1,0:T(8,128)(2,1)} %get-tuple-element.4.x_ref, f32[4,256]{1,0:T(4,128)S(1)} %copy-done.1), custom_call_target="tpu_custom_call" | custom-call | tf_op jit(solution)/shard_map/gram/pallas_call | solution.py:438
Async XLA Ops:
  0.6 128.1 %copy-start = (s32[4096]{0:T(1024)S(1)}, s32[4096]{0:T(1024)}, u32[]{:S(2)}) copy-start(s32[4096]{0:T(1024)} %slots.1) | copy-start | bytes 49156
  128.7 0.7 copy-start.1

commit v3 on v2

--- a/solution.py
+++ b/solution.py
@@ -180,7 +180,7 @@
 
         lax.fori_loop(0, 16, body, 0)
 
-    def transform(chunk):
+    def transform(chunk, begin, end):
         def body(pair, carry):
             cols = fb[pl.ds(pl.multiple_of(pair * 256, 256), 256), :]
             for kt in range(4):
@@ -193,22 +193,23 @@
                 send[chunk, kt * 32:(kt + 1) * 32, pl.ds(pl.multiple_of(pair * 16, 16), 16), :] = both
             return carry
 
-        lax.fori_loop(0, NS_CHUNK // 2, body, 0)
+        lax.fori_loop(begin, end, body, 0)
 
     def own_copy(chunk):
         return pltpu.make_async_copy(
             send.at[chunk, me], xv.at[me, pl.ds(chunk * BLOCK, BLOCK)], own_sem.at[chunk])
 
-    def spread(chunk):
+    def spread(chunk, begin, end):
+        rows = (end - begin) * 2 * PARTS
+
         def one(i, g):
             pltpu.make_async_remote_copy(
-                src_ref=send.at[chunk, i * N_GRP + g],
-                dst_ref=xv.at[me, pl.ds(chunk * BLOCK, BLOCK)],
+                src_ref=send.at[chunk, i * N_GRP + g, pl.ds(begin * 2 * PARTS, rows)],
+                dst_ref=xv.at[me, pl.ds(chunk * BLOCK + begin * 2 * PARTS, rows)],
                 send_sem=send_sem.at[chunk], recv_sem=recv_sem.at[chunk],
                 device_id=(i, g), device_id_type=MESH).start()
 
         for_peers(one)
-        own_copy(chunk).start()
 
     chip = pl.ds(grp // 2 * 2, 2)
     every = pl.ds(0, 4)
@@ -272,11 +273,16 @@
                 raw_copy(1, part).start()
         if chunk == 0:
             tab_copy.wait()
-        transform(chunk)
-        if chunk == 0:
+            transform(chunk, 0, 2)
             steer_wait(2)
             steer_start(3)
-        spread(chunk)
+            spread(chunk, 0, 2)
+            transform(chunk, 2, 4)
+            spread(chunk, 2, 4)
+        else:
+            transform(chunk, 0, 4)
+            spread(chunk, 0, 4)
+        own_copy(chunk).start()
         if chunk == 1:
             steer_wait(3)
             steer_start(4)

time: 143 us -> 149 us (1.042)
  Pallas kernels: 142 us -> 147 us
    pallas_call x1, Pallas kernels: 128 us -> 133 us  [per_device(): pl.pallas_call(channel_kernel, out_shape=(jax.ShapeDtypeStruct((COUNT, CH...]
where the time goes in v3:
time: 149 us; the launch traced here: 148 us
  Pallas kernels  147 us (99%)
    pallas_call x1, Pallas kernels, per_device(): pl.pallas_call(channel_kernel, out_shape=(jax.ShapeDtypeStruct((COUNT, CH...  133 us
    pallas_call x1, Pallas kernels, per_device(): pl.pallas_call(gram_kernel, out_shape=(jax.ShapeDtypeStruct((2, CH_DEV *...  13.7 us

profile of v3, /device:TPU:1, one launch (start us, length us, event | category | flops | bytes accessed | tf_op | source)
XLA Modules:
  0.0 148.3 jit_solution(17562631572116987978)
XLA Ops:
  0.6 0.0 copy-start
  0.6 133.3 %channelize.1 = (bf16[128,256,128]{2,1,0:T(8,128)(2,1)}, f32[4,256]{1,0:T(4,128)}) custom-call(bf16[32,268288]{1,0:T(8,128)(2,1)} %raw.1, bf16[1024,2048]{1,0:T(8,128)(2,1)} %constant.4.clone.table, f32[4,2048]{1,0:T(4,128)} %constant.5.clone.proto, s32[32,256]{1,0:T(8,128)} %bitcast.1), custom_call_target="tpu_custom_call" | custom-call | tf_op jit(solution)/shard_map/channelize/pallas_call | solution.py:415
  134.0 0.0 copy-done
  134.0 0.0 copy-start.1
  134.0 0.7 copy-done.1
  134.7 13.7 %gram.1 = (f32[2,256,4096]{2,1,0:T(8,128)}, f32[4,256]{1,0:T(4,128)}) custom-call(s32[4096]{0:T(1024)S(1)} %copy-done, bf16[128,256,128]{2,1,0:T(8,128)(2,1)} %get-tuple-element.4.x_ref, f32[4,256]{1,0:T(4,128)S(1)} %copy-done.1), custom_call_target="tpu_custom_call" | custom-call | tf_op jit(solution)/shard_map/gram/pallas_call | solution.py:444
Async XLA Ops:
  0.6 133.3 %copy-start = (s32[4096]{0:T(1024)S(1)}, s32[4096]{0:T(1024)}, u32[]{:S(2)}) copy-start(s32[4096]{0:T(1024)} %slots.1) | copy-start | bytes 49156
  134.0 0.7 copy-start.1
